TPU v7x, 128 devices: a whole 4x4x4 slice. The times are simulated.
128 devices in a mesh: dp: 16 (over y, z), expert: 8 (over x, core).
Axes of the slice: x: 4, y: 4, z: 4, core: 2. Of those that a mesh axis runs over, the one named last changes fastest.
Arguments:
- grad_out: bfloat16 [16384, 6144], P(('dp', 'expert')), may hold values from -6 to 6
- routes: int32 [16384, 2], P(('dp', 'expert')), may hold values from 0 to 31, all different within a row; in each aligned block of 128 rows (0 to 127, 128 to 255, ...) at most 9 rows name the same one
- loss_weight: int32 [16384], P(('dp', 'expert')), may hold values from 1 to 4
- saved_input: bfloat16 [32, 1152, 6144], P('dp', None, 'expert'), may hold values from -6 to 6
- saved_gate: bfloat16 [32, 1152, 1024], P('dp', None, 'expert'), may hold values from -8 to 8
- saved_up: bfloat16 [32, 1152, 1024], P('dp', None, 'expert'), may hold values from -6 to 6
- w_gate: bfloat16 [32, 6144, 1024], P('dp', 'expert'), may hold values from -0.1875 to 0.1875
- w_up: bfloat16 [32, 6144, 1024], P('dp', 'expert'), may hold values from -0.1875 to 0.1875
- w_down: bfloat16 [32, 1024, 6144], P('dp', None, 'expert'), may hold values from -0.078125 to 0.078125
Outputs:
- grad_input: bfloat16 [16384, 6144], P(('dp', 'expert'))
- grad_gate: bfloat16 [32, 6144, 1024], P('dp', 'expert')
- grad_up: bfloat16 [32, 6144, 1024], P('dp', 'expert')
- grad_down: bfloat16 [32, 1024, 6144], P('dp', None, 'expert')
Inputs may be any that keep to these rules, and one draw needn't show every extreme that they name: `routes`: each row names two different experts; among the rows of one device no expert is named more than 9 times, and some device names some expert exactly 9 times.
All inputs are finite; a program needn't handle non-finite values.
Results may differ from a plain program's by a relative error of at most 0.0061.
Values may be sent and summed in bfloat16 or wider, within the bound.
No kernel may reach another device: no remote copies, remote signals or barrier semaphores. Data moves between devices by JAX's collectives and lax.ppermute only.
A program may use at most 192 MiB of HBM per device.

v0:
```python
import jax
import jax.numpy as jnp
from jax import lax
from jax.sharding import PartitionSpec as P


def body(grad_out, routes, loss_weight, saved_input, saved_gate, saved_up, w_gate, w_up, w_down):
    groups = lax.axis_size("dp")
    splits = lax.axis_size("expert")
    local_experts = w_gate.shape[0]
    experts_all = local_experts * groups
    tokens_here = grad_out.shape[0]
    width = grad_out.shape[1]
    slice_width = width // splits
    slots_all = saved_input.shape[1]
    capacity = slots_all // (groups * splits)
    scaled = (
        grad_out.astype(jnp.float32) * loss_weight.astype(jnp.float32)[:, None] * 0.25
    ).astype(jnp.bfloat16)
    chosen = routes.reshape(-1)
    onehot = (chosen[:, None] == jnp.arange(experts_all, dtype=jnp.int32)[None, :]).astype(
        jnp.int32
    )
    before = jnp.cumsum(onehot, axis=0) - onehot
    rank = jnp.sum(before * onehot, axis=1)
    dest_row = (chosen % local_experts * groups + chosen // local_experts) * capacity + rank
    marks = (
        dest_row[:, None] == jnp.arange(experts_all * capacity, dtype=jnp.int32)[None, :]
    ).astype(jnp.float32)
    placed = jnp.sum(marks.reshape(tokens_here, 2, experts_all * capacity), axis=1).astype(
        jnp.bfloat16
    )
    outgoing = jnp.einsum("tr,td->rd", placed, scaled, preferred_element_type=jnp.float32).astype(
        jnp.bfloat16
    )
    ordered = outgoing.reshape(local_experts, groups, capacity, splits, slice_width)
    ordered = ordered.transpose(0, 1, 3, 2, 4).reshape(
        local_experts, groups * splits, capacity, slice_width
    )
    arrived = lax.all_to_all(ordered, ("dp", "expert"), split_axis=1, concat_axis=1, tiled=True)
    dispatched = arrived.reshape(local_experts, slots_all, slice_width)
    partial_value = jnp.einsum(
        "esd,ehd->esh", dispatched, w_down, preferred_element_type=jnp.float32
    )
    dhidden = lax.psum(partial_value, "expert")
    gates_all, ups_all = (
        lax.all_gather(saved_gate, "expert", axis=2, tiled=True),
        lax.all_gather(saved_up, "expert", axis=2, tiled=True),
    )
    gvals = gates_all.astype(jnp.float32)
    uvals = ups_all.astype(jnp.float32)
    sig = jax.nn.sigmoid(gvals)
    act = gvals * sig
    hidden = (act * uvals).astype(jnp.bfloat16)
    dgate = (dhidden * uvals * sig * (1.0 + gvals * (1.0 - sig))).astype(jnp.bfloat16)
    dup = (dhidden * act).astype(jnp.bfloat16)
    hidden, dgate, dup = (hidden, dgate, dup)
    grad_down = jnp.einsum(
        "esh,esd->ehd", hidden, dispatched, preferred_element_type=jnp.float32
    ).astype(jnp.bfloat16)
    grad_gate = jnp.einsum(
        "esd,esh->edh", saved_input, dgate, preferred_element_type=jnp.float32
    ).astype(jnp.bfloat16)
    grad_up = jnp.einsum(
        "esd,esh->edh", saved_input, dup, preferred_element_type=jnp.float32
    ).astype(jnp.bfloat16)
    slot_grad = jnp.einsum("esh,edh->esd", dgate, w_gate, preferred_element_type=jnp.float32)
    slot_grad = slot_grad + jnp.einsum(
        "esh,edh->esd", dup, w_up, preferred_element_type=jnp.float32
    )
    slot_grad = slot_grad.astype(jnp.bfloat16)
    leaving = slot_grad.reshape(local_experts, groups * splits, capacity, slice_width)
    returned = lax.all_to_all(leaving, ("dp", "expert"), split_axis=1, concat_axis=1, tiled=True)
    returned = returned.reshape(local_experts, groups, splits, capacity, slice_width).transpose(
        0, 1, 3, 2, 4
    )
    returned = returned.reshape(experts_all * capacity, width)
    grad_input = jnp.einsum(
        "tr,rd->td", placed, returned, preferred_element_type=jnp.float32
    ).astype(jnp.bfloat16)
    return (grad_input, grad_gate, grad_up, grad_down)


def solution(mesh):
    return jax.shard_map(
        body,
        mesh=mesh,
        in_specs=(
            P(("dp", "expert"), None),
            P(("dp", "expert"), None),
            P(("dp", "expert")),
            P("dp", None, "expert"),
            P("dp", None, "expert"),
            P("dp", None, "expert"),
            P("dp", "expert", None),
            P("dp", "expert", None),
            P("dp", None, "expert"),
        ),
        out_specs=(
            P(("dp", "expert"), None),
            P("dp", "expert", None),
            P("dp", "expert", None),
            P("dp", None, "expert"),
        ),
        check_vma=False,
    )
```

profile of v0, /device:TPU:1, one launch (start us, length us, event | category | flops | bytes accessed | tf_op | source)
XLA Modules:
  0.0 385.4 jit_solution(1867682180642988697)
XLA Ops:
  7.2 0.0 copy-start
  7.2 0.0 all-reduce.2.cloned.1.call-start
  7.2 1.6 copy.105
  8.8 1.0 eq.45
  9.8 1.0 eq.41
  10.7 0.7 convert_element_type.67
  11.4 0.6 fusion.25
  12.0 1.9 reduce-window.6
  13.9 0.9 slice_reduce_fusion
  14.9 0.9 fusion.24
  15.8 0.8 reduce_sum.21
  16.5 0.9 copy.108
  17.4 0.7 multiply_add_fusion
  18.2 0.0 copy-start.4
  18.2 2.6 convolution_convert_fusion
  20.8 0.0 copy-done.4
  20.8 1.0 copy.124
  21.8 0.4 copy.134
  22.3 3.6 copy.110
  25.9 0.0 copy-start.6
  25.9 57.3 %all_to_all.10 = bf16[2,128,9,768]{3,0,2,1:T(2,128)(2,1)S(1)} all-to-all(bf16[2,128,9,768]{3,0,2,1:T(2,128)(2,1)S(1)} %copy.110), channel_id=1, replica_groups=mesh['dp'=16,'expert'=8] {'dp','expert'}, dimensions={1} | all-to-all | bytes 7077888 | tf_op jit(solution)/shard_map/all_to_all | solution.py:40
  83.3 1.9 copy-done.3
  85.1 6.2 %fusion.11 = f32[2,1152,1024]{2,1,0:T(8,128)} fusion(bf16[2,1024,768]{2,1,0:T(8,128)(2,1)S(1)} %copy-done.6, bf16[2,1152,768]{2,0,1:T(2,128)(2,1)S(1)} %bitcast.56), kind=kOutput, calls=%fused_computation.23 | convolution fusion | flops 3623878656 | bytes 16121856 | tf_op jit(solution)/shard_map/esd,ehd->esh/dot_general | solution.py:42
  91.3 0.0 all-reduce.2.cloned.1.call-update
  91.3 0.0 all-gather.5.cloned.1.call-start
  91.4 0.7 all-gather.5.cloned.1.call-update
  92.1 0.2 all-gather.3.cloned.1.call-start
  92.3 0.5 all-gather.3.cloned.1.call-update
  92.8 108.4 %all-reduce.2.cloned.1.call-done = f32[2,1152,1024]{2,1,0:T(8,128)} async-done(((f32[2,1152,1024]{2,1,0:T(8,128)}), f32[2,1152,1024]{2,1,0:T(8,128)}) %all-reduce.2.cloned.1.call-update) | async-done | bytes 9437200 | tf_op jit(solution)/shard_map/psum | solution.py:45
  201.2 40.5 %all-gather.5.cloned.1.call-done = bf16[2,1152,1024]{2,1,0:T(8,128)(2,1)} async-done(((bf16[2,1152,128]{2,1,0:T(8,128)(2,1)}), bf16[2,1152,1024]{2,1,0:T(8,128)(2,1)}) %all-gather.5.cloned.1.call-update) | async-done | bytes 4718608 | tf_op jit(solution)/shard_map/all_gather | solution.py:47
  241.8 41.0 %all-gather.3.cloned.1.call-done = bf16[2,1152,1024]{2,1,0:T(8,128)(2,1)} async-done(((bf16[2,1152,128]{2,1,0:T(8,128)(2,1)}), bf16[2,1152,1024]{2,1,0:T(8,128)(2,1)}) %all-gather.3.cloned.1.call-update) | async-done | bytes 4718608 | tf_op jit(solution)/shard_map/all_gather | solution.py:48
  282.7 9.0 %multiply_convert_fusion = (bf16[2,1152,1024]{2,1,0:T(8,128)(2,1)S(1)}, bf16[2,1152,1024]{2,1,0:T(8,128)(2,1)S(1)}) fusion(f32[2,1152,1024]{2,1,0:T(8,128)} %all-reduce.2.cloned.1.call-done, bf16[2,1152,1024]{2,1,0:T(8,128)(2,1)} %all-gather.5.cloned.1.call-done, bf16[2,1152,1024]{2,1,0:T(8,128)(2,1)} %all-gather.3.cloned.1.call-done), kind=kLoop, calls=%fused_computation.13 | loop fusion | flops 35389440 | bytes 28311552 | tf_op jit(solution)/shard_map/convert_element_type | solution.py:56
  291.8 0.0 copy-start.8
  291.8 5.9 %fusion.30 = f32[2,1152,768]{2,1,0:T(8,128)} fusion(bf16[2,1152,1024]{2,1,0:T(8,128)(2,1)S(1)} %get-tuple-element.29, bf16[2,768,1024]{2,1,0:T(8,128)(2,1)S(1)} %copy-done.7), kind=kOutput, calls=%fused_computation.51 | convolution fusion | flops 3623878656 | bytes 14942208 | tf_op jit(solution)/shard_map/esh,edh->esd/dot_general | solution.py:67
  297.8 0.4 copy-done.2
  298.2 6.1 %add_convert_fusion = bf16[2,1152,768]{2,1,0:T(8,128)(2,1)S(1)} fusion(f32[2,1152,768]{2,1,0:T(8,128)} %fusion.30, bf16[2,1152,1024]{2,1,0:T(8,128)(2,1)S(1)} %get-tuple-element.28, bf16[2,768,1024]{2,1,0:T(8,128)(2,1)S(1)} %copy-done.8), kind=kOutput, calls=%fused_computation.16 | convolution fusion | flops 3627417600 | bytes 18481152 | tf_op jit(solution)/shard_map/esh,edh->esd/dot_general | solution.py:68
  304.3 13.9 %copy.112 = bf16[2,1152,768]{2,0,1:T(2,128)(2,1)} copy(bf16[2,1152,768]{2,1,0:T(8,128)(2,1)S(1)} %add_convert_fusion) | data formatting | bytes 7077888 | tf_op jit(solution)/shard_map/convert_element_type | solution.py:71
  318.2 9.3 %all-to-all-start.1 = ((bf16[2,128,9,768]{3,0,2,1:T(2,128)(2,1)}), bf16[2,128,9,768]{3,0,2,1:T(2,128)(2,1)}, u32[]{:S(2)}, u32[]{:S(2)}) async-start(bf16[2,128,9,768]{3,0,2,1:T(2,128)(2,1)} %bitcast.52), calls=%async_computation.1 | async-start | bytes 7077888 | tf_op jit(solution)/shard_map/all_to_all | solution.py:73
  327.5 9.4 %convert_bitcast_fusion = bf16[2,768,1024]{1,2,0:T(8,128)(2,1)} fusion(bf16[2,1152,1024]{2,1,0:T(8,128)(2,1)} %copy-done.2, bf16[2,1152,768]{2,1,0:T(8,128)(2,1)S(1)} %copy-done), kind=kOutput, calls=%fused_computation.19 | convolution fusion | flops 3625451520 | bytes 11403264 | tf_op jit(solution)/shard_map/esd,esh->edh/dot_general | solution.py:64
  337.0 4.6 %copy.119 = bf16[2,768,1024]{2,1,0:T(8,128)(2,1)} copy(bf16[2,768,1024]{1,2,0:T(8,128)(2,1)} %convert_bitcast_fusion) | data formatting | bytes 6291456
  341.6 9.4 %convert_bitcast_fusion.1 = bf16[2,768,1024]{1,2,0:T(8,128)(2,1)} fusion(bf16[2,1152,1024]{2,1,0:T(8,128)(2,1)} %copy-done.1, bf16[2,1152,768]{2,1,0:T(8,128)(2,1)S(1)} %copy-done), kind=kOutput, calls=%fused_computation.20 | convolution fusion | flops 3625451520 | bytes 11403264 | tf_op jit(solution)/shard_map/esd,esh->edh/dot_general | solution.py:61
  351.0 4.6 %copy.118 = bf16[2,768,1024]{2,1,0:T(8,128)(2,1)} copy(bf16[2,768,1024]{1,2,0:T(8,128)(2,1)} %convert_bitcast_fusion.1) | data formatting | bytes 6291456
  355.6 12.1 %fusion.13 = bf16[2,1024,768]{2,1,0:T(8,128)(2,1)} fusion(bf16[2,1152,768]{2,0,1:T(2,128)(2,1)} %bitcast.57, bf16[2,1152,1024]{2,1,0:T(8,128)(2,1)} %all-gather.3.cloned.1.call-done, bf16[2,1152,1024]{2,1,0:T(8,128)(2,1)} %all-gather.5.cloned.1.call-done), kind=kOutput, calls=%fused_computation.25 | convolution fusion | flops 3644325888 | bytes 16121856 | tf_op jit(solution)/shard_map/esh,esd->ehd/dot_general | solution.py:58
  367.8 5.5 %all-to-all-done.1 = bf16[2,128,9,768]{3,0,2,1:T(2,128)(2,1)} async-done(((bf16[2,128,9,768]{3,0,2,1:T(2,128)(2,1)}), bf16[2,128,9,768]{3,0,2,1:T(2,128)(2,1)}, u32[]{:S(2)}, u32[]{:S(2)}) %all-to-all-start.1) | async-done | bytes 3538976 | tf_op jit(solution)/shard_map/all_to_all | solution.py:73
  373.2 2.5 copy.113
  375.7 0.0 copy-start.5
  375.7 1.0 copy.125
  376.7 2.2 convolution_convert_fusion.1
  (13 shorter events, 0.1 us)
Async XLA Ops:
  7.2 320.4 %copy-start = (bf16[2,1152,768]{2,1,0:T(8,128)(2,1)S(1)}, bf16[2,1152,768]{2,1,0:T(8,128)(2,1)}, u32[]{:S(2)}) copy-start(bf16[2,1152,768]{2,1,0:T(8,128)(2,1)} %param.12) | copy-start | bytes 10616836
  7.2 194.1 %all-reduce.2.cloned.1.call-start = ((), (), s32[]{:S(2)}) async-start(), calls=%async_computation.2 | async-start | bytes 18874368 | tf_op jit(solution)/shard_map/psum | solution.py:45
  18.2 2.6 copy-start.4
  25.9 59.2 %copy-start.6 = (bf16[2,1024,768]{2,1,0:T(8,128)(2,1)S(1)}, bf16[2,1024,768]{2,1,0:T(8,128)(2,1)}, u32[]{:S(2)}) copy-start(bf16[2,1024,768]{2,1,0:T(8,128)(2,1)} %param.17) | copy-start | bytes 9437188
  83.2 1.9 copy-start.3
  91.3 150.4 %all-gather.5.cloned.1.call-start = ((), (), s32[]{:S(2)}) async-start(), calls=%async_computation.4 | async-start | bytes 5308416 | tf_op jit(solution)/shard_map/all_gather | solution.py:47
  92.1 190.6 %all-gather.3.cloned.1.call-start = ((), (), s32[]{:S(2)}) async-start(), calls=%async_computation.3 | async-start | bytes 5308416 | tf_op jit(solution)/shard_map/all_gather | solution.py:48
  282.7 9.1 %copy-start.7 = (bf16[2,768,1024]{2,1,0:T(8,128)(2,1)S(1)}, bf16[2,768,1024]{2,1,0:T(8,128)(2,1)}, u32[]{:S(2)}) copy-start(bf16[2,768,1024]{2,1,0:T(8,128)(2,1)} %param.15) | copy-start | bytes 9437188
  291.8 6.0 %copy-start.1 = (bf16[2,1152,1024]{2,1,0:T(8,128)(2,1)}, bf16[2,1152,1024]{2,1,0:T(8,128)(2,1)S(1)}, u32[]{:S(2)}) copy-start(bf16[2,1152,1024]{2,1,0:T(8,128)(2,1)S(1)} %get-tuple-element.29) | copy-start | bytes 14155780
  291.8 6.4 %copy-start.2 = (bf16[2,1152,1024]{2,1,0:T(8,128)(2,1)}, bf16[2,1152,1024]{2,1,0:T(8,128)(2,1)S(1)}, u32[]{:S(2)}) copy-start(bf16[2,1152,1024]{2,1,0:T(8,128)(2,1)S(1)} %get-tuple-element.28) | copy-start | bytes 14155780
  291.8 6.4 %copy-start.8 = (bf16[2,768,1024]{2,1,0:T(8,128)(2,1)S(1)}, bf16[2,768,1024]{2,1,0:T(8,128)(2,1)}, u32[]{:S(2)}) copy-start(bf16[2,768,1024]{2,1,0:T(8,128)(2,1)} %param.16) | copy-start | bytes 9437188
  318.2 55.0 %all-to-all-start.1 = ((bf16[2,128,9,768]{3,0,2,1:T(2,128)(2,1)}), bf16[2,128,9,768]{3,0,2,1:T(2,128)(2,1)}, u32[]{:S(2)}, u32[]{:S(2)}) async-start(bf16[2,128,9,768]{3,0,2,1:T(2,128)(2,1)} %bitcast.52), calls=%async_computation.1 | async-start | bytes 7077888 | tf_op jit(solution)/shard_map/all_to_all | solution.py:73
  375.7 1.0 copy-start.5
Sparse Core Ops, SparseCore 0:
  91.5 109.7 all-reduce.1
  202.9 38.8 all-gather.4
  243.5 39.2 all-gather.2
where the time goes:
time: 386 us; the launch traced here: 385 us
  waiting for transfers between devices  197 us (51%)
  blocking collectives  57.3 us (15%)
  matrix products  54 us (14%)
  local copies, waits for them, and re-layouts  40.1 us (10%)
  other arithmetic  13.9 us (4%)
  between operations  13.9 us (4%)
  starting transfers between devices  9.56 us (2%)
    psum x1, waiting for transfers between devices, body(): dhidden = lax.psum(partial_value, 'expert')  108 us
    all_to_all x1, blocking collectives, body(): lax.all_to_all(ordered, ('dp', 'expert'), split_axis=1, concat_axis=1, ti...  57.3 us
    all_gather x1, waiting for transfers between devices, body(): lax.all_gather(saved_up, 'expert', axis=2, tiled=True)  41 us
    all_gather x1, waiting for transfers between devices, body(): lax.all_gather(saved_gate, 'expert', axis=2, tiled=True)  40.5 us
    unnamed x23, local copies, waits for them, and re-layouts  15.2 us
    convert_element_type x1, local copies, waits for them, and re-layouts, body(): slot_grad = slot_grad.astype(jnp.bfloat16)  13.9 us
    dot_general x1, matrix products, body(): jnp.einsum('esh,esd->ehd', hidden, dispatched, preferred_element_type=jnp...  12.1 us
    dot_general x1, matrix products, body(): jnp.einsum('esd,esh->edh', saved_input, dup, preferred_element_type=jnp.f...  9.43 us
  transfers between devices with their start and end apart: 4, of which 4 were waited for; matrix products, arithmetic and copies ran while one was open for 10% of the time, Pallas kernels for 0%

commit v1 on v0

--- a/solution.py
+++ b/solution.py
@@ -2,6 +2,19 @@
 import jax.numpy as jnp
 from jax import lax
 from jax.sharding import PartitionSpec as P
+
+
+def ring_gather(value, axis, dim):
+    ways = lax.axis_size(axis)
+    up = [(d, (d + 1) % ways) for d in range(ways)]
+    down = [(d, (d - 1) % ways) for d in range(ways)]
+    earlier, later = ([value], [value])
+    for _ in range(ways // 2):
+        earlier.append(lax.ppermute(earlier[-1], axis, up))
+    for _ in range((ways - 1) // 2):
+        later.append(lax.ppermute(later[-1], axis, down))
+    line = jnp.concatenate([*earlier[::-1], *later[1:]], axis=dim)
+    return jnp.roll(line, (lax.axis_index(axis) - ways // 2) * value.shape[dim], axis=dim)
 
 
 def body(grad_out, routes, loss_weight, saved_input, saved_gate, saved_up, w_gate, w_up, w_down):
@@ -45,7 +58,7 @@
     dhidden = lax.psum(partial_value, "expert")
     gates_all, ups_all = (
         lax.all_gather(saved_gate, "expert", axis=2, tiled=True),
-        lax.all_gather(saved_up, "expert", axis=2, tiled=True),
+        ring_gather(saved_up, "expert", 2),
     )
     gvals = gates_all.astype(jnp.float32)
     uvals = ups_all.astype(jnp.float32)

time: 386 us -> 365 us (0.946)
  waiting for transfers between devices: 197 us -> 132 us
  local copies, waits for them, and re-layouts: 40.1 us -> 68.4 us
  starting transfers between devices: 9.56 us -> 23.5 us
    psum x1, waiting for transfers between devices: 108 us -> 39.7 us  [body(): dhidden = lax.psum(partial_value, 'expert')]
    ppermute x0 -> x7, waiting for transfers between devices: none -> 46.1 us  [the longest x4 45.6 us: ring_gather(): earlier.append(lax.ppermute(earlier[-1], axis, up))]
    all_gather x1 -> x0, waiting for transfers between devices: 41 us -> none  [body(): lax.all_gather(saved_up, 'expert', axis=2, tiled=True)]
    unnamed x23 -> x48, local copies, waits for them, and re-layouts: 15.2 us -> 42.5 us
    ppermute x0 -> x7, starting transfers between devices: none -> 13.9 us  [the longest x4 8.51 us: ring_gather(): earlier.append(lax.ppermute(earlier[-1], axis, up))]
  transfers between devices with their start and end apart: 4 -> 10, of which waited for: 4 -> 8; matrix products, arithmetic and copies ran while one was open for 10% -> 18% of each run, Pallas kernels for 0% -> 0%
where the time goes in v1:
time: 365 us; the launch traced here: 364 us
  waiting for transfers between devices  132 us (36%)
  local copies, waits for them, and re-layouts  68.4 us (19%)
  blocking collectives  57.3 us (16%)
  matrix products  54 us (15%)
  starting transfers between devices  23.5 us (6%)
  between operations  14.2 us (4%)
  other arithmetic  13.9 us (4%)
    all_to_all x1, blocking collectives, body(): lax.all_to_all(ordered, ('dp', 'expert'), split_axis=1, concat_axis=1, ti...  57.3 us
    ppermute x4, waiting for transfers between devices, ring_gather(): earlier.append(lax.ppermute(earlier[-1], axis, up))  45.6 us
    unnamed x48, local copies, waits for them, and re-layouts  42.5 us
    all_gather x1, waiting for transfers between devices, body(): lax.all_gather(saved_gate, 'expert', axis=2, tiled=True)  40.5 us
    psum x1, waiting for transfers between devices, body(): dhidden = lax.psum(partial_value, 'expert')  39.7 us
    convert_element_type x1, local copies, waits for them, and re-layouts, body(): slot_grad = slot_grad.astype(jnp.bfloat16)  14 us
    dot_general x1, matrix products, body(): jnp.einsum('esh,esd->ehd', hidden, dispatched, preferred_element_type=jnp...  12.1 us
    dot_general x1, matrix products, body(): jnp.einsum('esd,esh->edh', saved_input, dgate, preferred_element_type=jnp...  9.43 us
  transfers between devices with their start and end apart: 10, of which 8 were waited for; matrix products, arithmetic and copies ran while one was open for 18% of the time, Pallas kernels for 0%

profile of v1, /device:TPU:1, one launch (start us, length us, event | category | flops | bytes accessed | tf_op | source)
XLA Modules:
  0.0 363.7 jit_solution(3476524283738627004)
XLA Ops:
  7.2 1.6 copy.105
  8.8 1.0 eq.48
  9.8 1.0 eq.44
  11.4 1.9 reduce-window.6
  18.2 2.6 convolution_convert_fusion
  20.8 1.0 copy.124
  22.3 3.6 %copy.110 = bf16[2,128,9,768]{3,0,2,1:T(2,128)(2,1)S(1)} copy(bf16[2,128,9,768]{3,1,2,0:T(8,128)(2,1)S(1)} %bitcast.54) | data formatting | bytes 7077888 | tf_op jit(solution)/shard_map/reshape | solution.py:50
  25.9 57.3 %all_to_all.10 = bf16[2,128,9,768]{3,0,2,1:T(2,128)(2,1)S(1)} all-to-all(bf16[2,128,9,768]{3,0,2,1:T(2,128)(2,1)S(1)} %copy.110), channel_id=1, replica_groups=mesh['dp'=16,'expert'=8] {'dp','expert'}, dimensions={1} | all-to-all | bytes 7077888 | tf_op jit(solution)/shard_map/all_to_all | solution.py:53
  83.2 1.7 copy-done.3
  85.0 6.2 %fusion.12 = f32[2,1152,1024]{2,1,0:T(8,128)} fusion(bf16[2,1024,768]{2,1,0:T(8,128)(2,1)S(1)} %copy-done.11, bf16[2,1152,768]{2,0,1:T(2,128)(2,1)S(1)} %bitcast.56), kind=kOutput, calls=%fused_computation.24 | convolution fusion | flops 3623878656 | bytes 16121856 | tf_op jit(solution)/shard_map/esd,ehd->esh/dot_general | solution.py:55
  92.0 1.1 collective-permute-start
  93.0 11.5 %collective-permute-done = bf16[2,1152,128]{2,1,0:T(8,128)(2,1)S(1)} collective-permute-done((bf16[2,1152,128]{2,1,0:T(8,128)(2,1)}, bf16[2,1152,128]{2,1,0:T(8,128)(2,1)S(1)}, u32[]{:S(2)}, u32[]{:S(2)}) %collective-permute-start) | collective-permute-done | bytes 589856 | tf_op jit(solution)/shard_map/ppermute | solution.py:13
  105.4 2.4 collective-permute-start.1
  108.5 12.5 %collective-permute-done.1 = bf16[2,1152,128]{2,1,0:T(8,128)(2,1)S(1)} collective-permute-done((bf16[2,1152,128]{2,1,0:T(8,128)(2,1)S(1)}, bf16[2,1152,128]{2,1,0:T(8,128)(2,1)S(1)}, u32[]{:S(2)}, u32[]{:S(2)}) %collective-permute-start.1) | collective-permute-done | bytes 589856 | tf_op jit(solution)/shard_map/ppermute | solution.py:13
  121.8 2.5 collective-permute-start.2
  124.3 2.0 collective-permute-start.5
  126.2 11.3 %collective-permute-done.2 = bf16[2,1152,128]{2,1,0:T(8,128)(2,1)} collective-permute-done((bf16[2,1152,128]{2,1,0:T(8,128)(2,1)S(1)}, bf16[2,1152,128]{2,1,0:T(8,128)(2,1)}, u32[]{:S(2)}, u32[]{:S(2)}) %collective-permute-start.2) | collective-permute-done | bytes 589856 | tf_op jit(solution)/shard_map/ppermute | solution.py:13
  137.5 2.6 collective-permute-start.3
  140.6 2.7 collective-permute-start.6
  143.3 10.3 %collective-permute-done.3 = bf16[2,1152,128]{2,1,0:T(8,128)(2,1)} collective-permute-done((bf16[2,1152,128]{2,1,0:T(8,128)(2,1)}, bf16[2,1152,128]{2,1,0:T(8,128)(2,1)}, u32[]{:S(2)}, u32[]{:S(2)}) %collective-permute-start.3) | collective-permute-done | bytes 589856 | tf_op jit(solution)/shard_map/ppermute | solution.py:13
  153.6 2.0 constant_dynamic-update-slice_fusion.15
  155.6 2.1 constant_dynamic-update-slice_fusion.14
  157.7 2.0 constant_dynamic-update-slice_fusion.13
  159.7 2.0 constant_dynamic-update-slice_fusion.12
  161.7 2.0 constant_dynamic-update-slice_fusion.11
  163.7 2.0 constant_dynamic-update-slice_fusion.10
  165.7 2.0 constant_dynamic-update-slice_fusion.9
  168.5 2.0 constant_dynamic-update-slice_fusion.7
  170.5 2.0 constant_dynamic-update-slice_fusion.6
  172.6 0.9 constant_dynamic-update-slice_fusion.5
  175.3 2.1 constant_dynamic-update-slice_fusion.2
  177.4 2.0 constant_dynamic-update-slice_fusion.1
  180.4 39.7 %all-reduce.2.cloned.1.call-done = f32[2,1152,1024]{2,1,0:T(8,128)} async-done(((f32[2,1152,1024]{2,1,0:T(8,128)}), f32[2,1152,1024]{2,1,0:T(8,128)}) %all-reduce.2.cloned.1.call-update) | async-done | bytes 9437200 | tf_op jit(solution)/shard_map/psum | solution.py:58
  220.1 40.5 %all-gather.2.cloned.1.call-done = bf16[2,1152,1024]{2,1,0:T(8,128)(2,1)} async-done(((bf16[2,1152,128]{2,1,0:T(8,128)(2,1)}), bf16[2,1152,1024]{2,1,0:T(8,128)(2,1)}) %all-gather.2.cloned.1.call-update) | async-done | bytes 4718608 | tf_op jit(solution)/shard_map/all_gather | solution.py:60
  260.6 9.1 %fusion.2 = (bf16[2,1152,1024]{2,1,0:T(8,128)(2,1)S(1)}, bf16[2,1152,1024]{2,1,0:T(8,128)(2,1)S(1)}) fusion(f32[2,1152,1024]{2,1,0:T(8,128)} %all-reduce.2.cloned.1.call-done, bf16[2,1152,1024]{2,1,0:T(8,128)(2,1)} %all-gather.2.cloned.1.call-done, bf16[2,1152,2048]{2,1,0:T(8,128)(2,1)} %constant_dynamic-update-slice_fusion, s32[]{:T(128)S(6)} %select_n.35), kind=kLoop, calls=%fused_computation.7 | loop fusion | flops 35389440 | bytes 28311556 | tf_op jit(solution)/shard_map/convert_element_type | solution.py:68
  269.8 5.9 %fusion.32 = f32[2,1152,768]{2,1,0:T(8,128)} fusion(bf16[2,1152,1024]{2,1,0:T(8,128)(2,1)S(1)} %get-tuple-element.29, bf16[2,768,1024]{2,1,0:T(8,128)(2,1)S(1)} %copy-done.12), kind=kOutput, calls=%fused_computation.69 | convolution fusion | flops 3623878656 | bytes 14942208 | tf_op jit(solution)/shard_map/esh,edh->esd/dot_general | solution.py:81
  276.1 6.1 %add_convert_fusion = bf16[2,1152,768]{2,1,0:T(8,128)(2,1)S(1)} fusion(f32[2,1152,768]{2,1,0:T(8,128)} %fusion.32, bf16[2,1152,1024]{2,1,0:T(8,128)(2,1)S(1)} %get-tuple-element.28, bf16[2,768,1024]{2,1,0:T(8,128)(2,1)S(1)} %copy-done.13), kind=kOutput, calls=%fused_computation.16 | convolution fusion | flops 3627417600 | bytes 18481152 | tf_op jit(solution)/shard_map/esh,edh->esd/dot_general | solution.py:80
  282.2 14.0 %copy.112 = bf16[2,1152,768]{2,0,1:T(2,128)(2,1)} copy(bf16[2,1152,768]{2,1,0:T(8,128)(2,1)S(1)} %add_convert_fusion) | data formatting | bytes 7077888 | tf_op jit(solution)/shard_map/convert_element_type | solution.py:84
  296.2 9.3 %all-to-all-start.1 = ((bf16[2,128,9,768]{3,0,2,1:T(2,128)(2,1)}), bf16[2,128,9,768]{3,0,2,1:T(2,128)(2,1)}, u32[]{:S(2)}, u32[]{:S(2)}) async-start(bf16[2,128,9,768]{3,0,2,1:T(2,128)(2,1)} %bitcast.52), calls=%async_computation.1 | async-start | bytes 7077888 | tf_op jit(solution)/shard_map/all_to_all | solution.py:86
  305.5 9.4 %convert_bitcast_fusion.1 = bf16[2,768,1024]{1,2,0:T(8,128)(2,1)} fusion(bf16[2,1152,1024]{2,1,0:T(8,128)(2,1)} %copy-done.2, bf16[2,1152,768]{2,1,0:T(8,128)(2,1)S(1)} %copy-done), kind=kOutput, calls=%fused_computation.21 | convolution fusion | flops 3625451520 | bytes 11403264 | tf_op jit(solution)/shard_map/esd,esh->edh/dot_general | solution.py:74
  314.9 4.6 %copy.118 = bf16[2,768,1024]{2,1,0:T(8,128)(2,1)} copy(bf16[2,768,1024]{1,2,0:T(8,128)(2,1)} %convert_bitcast_fusion.1) | data formatting | bytes 6291456
  319.5 9.4 %convert_bitcast_fusion = bf16[2,768,1024]{1,2,0:T(8,128)(2,1)} fusion(bf16[2,1152,1024]{2,1,0:T(8,128)(2,1)} %copy-done.1, bf16[2,1152,768]{2,1,0:T(8,128)(2,1)S(1)} %copy-done), kind=kOutput, calls=%fused_computation.20 | convolution fusion | flops 3625451520 | bytes 11403264 | tf_op jit(solution)/shard_map/esd,esh->edh/dot_general | solution.py:77
  329.0 4.6 %copy.119 = bf16[2,768,1024]{2,1,0:T(8,128)(2,1)} copy(bf16[2,768,1024]{1,2,0:T(8,128)(2,1)} %convert_bitcast_fusion) | data formatting | bytes 6291456
  333.6 12.1 %fusion.14 = bf16[2,1024,768]{2,1,0:T(8,128)(2,1)} fusion(bf16[2,1152,768]{2,0,1:T(2,128)(2,1)} %bitcast.57, bf16[2,1152,2048]{2,1,0:T(8,128)(2,1)} %constant_dynamic-update-slice_fusion, s32[]{:T(128)S(6)} %select_n.35, bf16[2,1152,1024]{2,1,0:T(8,128)(2,1)} %all-gather.2.cloned.1.call-done), kind=kOutput, calls=%fused_computation.26 | convolution fusion | flops 3644325888 | bytes 16121860 | tf_op jit(solution)/shard_map/esh,esd->ehd/dot_general | solution.py:71
  345.8 5.4 %all-to-all-done.1 = bf16[2,128,9,768]{3,0,2,1:T(2,128)(2,1)} async-done(((bf16[2,128,9,768]{3,0,2,1:T(2,128)(2,1)}), bf16[2,128,9,768]{3,0,2,1:T(2,128)(2,1)}, u32[]{:S(2)}, u32[]{:S(2)}) %all-to-all-start.1) | async-done | bytes 3538976 | tf_op jit(solution)/shard_map/all_to_all | solution.py:86
  351.2 2.5 copy.113
  353.7 1.0 copy.125
  354.7 2.2 convolution_convert_fusion.1
  (50 shorter events, 13.8 us)
Async XLA Ops:
  7.2 298.3 %copy-start = (bf16[2,1152,768]{2,1,0:T(8,128)(2,1)S(1)}, bf16[2,1152,768]{2,1,0:T(8,128)(2,1)}, u32[]{:S(2)}) copy-start(bf16[2,1152,768]{2,1,0:T(8,128)(2,1)} %param.12) | copy-start | bytes 10616836
  7.2 212.9 %all-reduce.2.cloned.1.call-start = ((), (), s32[]{:S(2)}) async-start(), calls=%async_computation.2 | async-start | bytes 18874368 | tf_op jit(solution)/shard_map/psum | solution.py:58
  17.5 3.3 copy-start.9
  22.2 62.7 %copy-start.11 = (bf16[2,1024,768]{2,1,0:T(8,128)(2,1)S(1)}, bf16[2,1024,768]{2,1,0:T(8,128)(2,1)}, u32[]{:S(2)}) copy-start(bf16[2,1024,768]{2,1,0:T(8,128)(2,1)} %param.17) | copy-start | bytes 9437188
  83.2 1.7 copy-start.3
  91.2 169.4 %all-gather.2.cloned.1.call-start = ((), (), s32[]{:S(2)}) async-start(), calls=%async_computation.3 | async-start | bytes 5308416 | tf_op jit(solution)/shard_map/all_gather | solution.py:60
  92.0 12.6 %collective-permute-start = (bf16[2,1152,128]{2,1,0:T(8,128)(2,1)}, bf16[2,1152,128]{2,1,0:T(8,128)(2,1)S(1)}, u32[]{:S(2)}, u32[]{:S(2)}) collective-permute-start(bf16[2,1152,128]{2,1,0:T(8,128)(2,1)} %param.14), channel_id=1, source_target_pairs={{0,1},{1,2},{2,3},{3,4},{4,5},{5,6},{6,7},{7,0},{8,9},{9,10},{10,1... | collective-permute-start | bytes 1769480 | tf_op jit(solution)/shard_map/ppermute | solution.py:13
  104.5 0.8 copy-start.5
  105.4 15.6 %collective-permute-start.1 = (bf16[2,1152,128]{2,1,0:T(8,128)(2,1)S(1)}, bf16[2,1152,128]{2,1,0:T(8,128)(2,1)S(1)}, u32[]{:S(2)}, u32[]{:S(2)}) collective-permute-start(bf16[2,1152,128]{2,1,0:T(8,128)(2,1)S(1)} %collective-permute-done), channel_id=1, source_target_pairs={{0,1},{1,2},{2,3},{3,4},{4,5},{5,6},{6,7},{7,0},{8,9},{9,10},{10,1... | collective-permute-start | bytes 1769480 | tf_op jit(solution)/shard_map/ppermute | solution.py:13
  107.7 16.5 %collective-permute-start.4 = (bf16[2,1152,128]{2,1,0:T(8,128)(2,1)}, bf16[2,1152,128]{2,1,0:T(8,128)(2,1)}, u32[]{:S(2)}, u32[]{:S(2)}) collective-permute-start(bf16[2,1152,128]{2,1,0:T(8,128)(2,1)} %param.14), channel_id=1, source_target_pairs={{0,7},{1,0},{2,1},{3,2},{4,3},{5,4},{6,5},{7,6},{8,15},{9,8},{10,9... | collective-permute-start | bytes 1769480 | tf_op jit(solution)/shard_map/ppermute | solution.py:15
  121.0 0.8 copy-start.7
  121.8 15.7 %collective-permute-start.2 = (bf16[2,1152,128]{2,1,0:T(8,128)(2,1)S(1)}, bf16[2,1152,128]{2,1,0:T(8,128)(2,1)}, u32[]{:S(2)}, u32[]{:S(2)}) collective-permute-start(bf16[2,1152,128]{2,1,0:T(8,128)(2,1)S(1)} %collective-permute-done.1), channel_id=1, source_target_pairs={{0,1},{1,2},{2,3},{3,4},{4,5},{5,6},{6,7},{7,0},{8,9},{9,10},{10,1... | collective-permute-start | bytes 1769480 | tf_op jit(solution)/shard_map/ppermute | solution.py:13
  124.3 16.3 %collective-permute-start.5 = (bf16[2,1152,128]{2,1,0:T(8,128)(2,1)}, bf16[2,1152,128]{2,1,0:T(8,128)(2,1)}, u32[]{:S(2)}, u32[]{:S(2)}) collective-permute-start(bf16[2,1152,128]{2,1,0:T(8,128)(2,1)} %collective-permute-done.4), channel_id=1, source_target_pairs={{0,7},{1,0},{2,1},{3,2},{4,3},{5,4},{6,5},{7,6},{8,15},{9,8},{10,9... | collective-permute-start | bytes 1769480 | tf_op jit(solution)/shard_map/ppermute | solution.py:15
  137.5 16.1 %collective-permute-start.3 = (bf16[2,1152,128]{2,1,0:T(8,128)(2,1)}, bf16[2,1152,128]{2,1,0:T(8,128)(2,1)}, u32[]{:S(2)}, u32[]{:S(2)}) collective-permute-start(bf16[2,1152,128]{2,1,0:T(8,128)(2,1)} %collective-permute-done.2), channel_id=1, source_target_pairs={{0,1},{1,2},{2,3},{3,4},{4,5},{5,6},{6,7},{7,0},{8,9},{9,10},{10,1... | collective-permute-start | bytes 1769480 | tf_op jit(solution)/shard_map/ppermute | solution.py:13
  140.1 32.5 %copy-start.8 = (bf16[2,1152,128]{2,1,0:T(8,128)(2,1)S(1)}, bf16[2,1152,128]{2,1,0:T(8,128)(2,1)}, u32[]{:S(2)}) copy-start(bf16[2,1152,128]{2,1,0:T(8,128)(2,1)} %copy-done.7) | copy-start | bytes 1769476
  140.1 33.4 %copy-start.6 = (bf16[2,1152,128]{2,1,0:T(8,128)(2,1)S(1)}, bf16[2,1152,128]{2,1,0:T(8,128)(2,1)}, u32[]{:S(2)}) copy-start(bf16[2,1152,128]{2,1,0:T(8,128)(2,1)} %copy-done.5) | copy-start | bytes 1769476
  140.6 27.1 %collective-permute-start.6 = (bf16[2,1152,128]{2,1,0:T(8,128)(2,1)}, bf16[2,1152,128]{2,1,0:T(8,128)(2,1)S(1)}, u32[]{:S(2)}, u32[]{:S(2)}) collective-permute-start(bf16[2,1152,128]{2,1,0:T(8,128)(2,1)} %collective-permute-done.5), channel_id=1, source_target_pairs={{0,7},{1,0},{2,1},{3,2},{4,3},{5,4},{6,5},{7,6},{8,15},{9,8},{10,9... | collective-permute-start | bytes 1769480 | tf_op jit(solution)/shard_map/ppermute | solution.py:15
  155.6 18.8 %copy-start.4 = (bf16[2,1152,128]{2,1,0:T(8,128)(2,1)S(1)}, bf16[2,1152,128]{2,1,0:T(8,128)(2,1)}, u32[]{:S(2)}) copy-start(bf16[2,1152,128]{2,1,0:T(8,128)(2,1)} %param.14) | copy-start | bytes 1769476
  260.6 9.1 %copy-start.12 = (bf16[2,768,1024]{2,1,0:T(8,128)(2,1)S(1)}, bf16[2,768,1024]{2,1,0:T(8,128)(2,1)}, u32[]{:S(2)}) copy-start(bf16[2,768,1024]{2,1,0:T(8,128)(2,1)} %param.16) | copy-start | bytes 9437188
  269.7 6.0 %copy-start.1 = (bf16[2,1152,1024]{2,1,0:T(8,128)(2,1)}, bf16[2,1152,1024]{2,1,0:T(8,128)(2,1)S(1)}, u32[]{:S(2)}) copy-start(bf16[2,1152,1024]{2,1,0:T(8,128)(2,1)S(1)} %get-tuple-element.29) | copy-start | bytes 14155780
  269.7 6.4 %copy-start.2 = (bf16[2,1152,1024]{2,1,0:T(8,128)(2,1)}, bf16[2,1152,1024]{2,1,0:T(8,128)(2,1)S(1)}, u32[]{:S(2)}) copy-start(bf16[2,1152,1024]{2,1,0:T(8,128)(2,1)S(1)} %get-tuple-element.28) | copy-start | bytes 14155780
  269.7 6.4 %copy-start.13 = (bf16[2,768,1024]{2,1,0:T(8,128)(2,1)S(1)}, bf16[2,768,1024]{2,1,0:T(8,128)(2,1)}, u32[]{:S(2)}) copy-start(bf16[2,768,1024]{2,1,0:T(8,128)(2,1)} %param.15) | copy-start | bytes 9437188
  296.2 55.0 %all-to-all-start.1 = ((bf16[2,128,9,768]{3,0,2,1:T(2,128)(2,1)}), bf16[2,128,9,768]{3,0,2,1:T(2,128)(2,1)}, u32[]{:S(2)}, u32[]{:S(2)}) async-start(bf16[2,128,9,768]{3,0,2,1:T(2,128)(2,1)} %bitcast.52), calls=%async_computation.1 | async-start | bytes 7077888 | tf_op jit(solution)/shard_map/all_to_all | solution.py:86
  351.2 3.5 copy-start.10
Sparse Core Ops, SparseCore 0:
  91.3 128.7 all-reduce.1
  221.8 38.8 all-gather.1
